TPU v7x, 32 devices: a whole 2x2x4 slice. The times are simulated.
32 devices in a mesh: parts: 2 (over y), plane: 4 (over z), band: 2 (over x), sub: 2 (over core).
Axes of the slice: x: 2, y: 2, z: 4, core: 2. Of those that a mesh axis runs over, the one named last changes fastest.
Arguments:
- coefficients: float32 [2, 2, 256, 128], P(None, None, ('parts', 'plane', 'band', 'sub')), parts along dimension 2, may hold values from -6 to 6
- potential: float32 [400, 192, 192], P(('parts', 'plane', 'sub')), parts along dimension 0, may hold values from -1 to 3
- stick_column: int32 [128], replicated, may hold values from 0 to 36863, as said below
- stick_length: int32 [128], replicated, may hold values from 0 to 97, as said below
- plane_start: int32 [9], replicated, may hold values from 0 to 192, as said below
Outputs:
- applied: float32 [2, 2, 256, 128], P(None, None, ('parts', 'plane', 'band', 'sub')), parts along dimension 2
There are 2 independent parts, one for each index of `parts`. A program takes and returns all parts, laid end to end along the dimension named above; an argument that names none is the same for every part. Nothing has to cross between parts.
Inputs may be any that keep to these rules, and one draw needn't show every extreme that they name: `stick_column`: distinct over all 128 slots; each is x * 192 + y for a column whose centred coordinates (x or x - 192, y or y - 192, the one of smaller size) lie within 48 of the anchor. `stick_length`: 0 marks an empty slot; a live stick whose column has centred coordinates (a, b) has length 2 * floor(sqrt(48^2 - a^2 - b^2)) + 1; on each device the live slots come first and number at least 4, and some device has all 8 live. `plane_start`: never falling, first entry 0, last 192; an owner holds at most 25 planes and some owner holds exactly 25.
All inputs are finite; a program needn't handle non-finite values.
Results may differ from a plain program's by a relative error of at most 0.00007.
Values sent between devices are 32-bit elements; how exact they have to be, the bound alone decides.
A program may use at most 64 MiB of HBM per device.

v0:
```python
import functools
import math

import jax
import jax.numpy as jnp
from jax import lax
from jax.experimental import pallas as pl
from jax.experimental.pallas import tpu as pltpu
from jax.sharding import PartitionSpec as P

LANES = 128
HALF = LANES // 2
SIN_TERMS = [(-1.0) ** k / math.factorial(2 * k + 1) for k in range(7)]
COS_TERMS = [(-1.0) ** k / math.factorial(2 * k) for k in range(8)]


def series(square, terms):
    total = jnp.full_like(square, terms[-1])
    for term in reversed(terms[:-1]):
        total = total * square + term
    return total


def phases(product, grid_size):
    turns = product * (1.0 / grid_size)
    rest = product - grid_size * jnp.floor(turns + 0.5)
    angle = rest * (math.pi / grid_size)
    square = angle * angle
    half_sin = angle * series(square, SIN_TERMS)
    half_cos = series(square, COS_TERMS)
    return 1.0 - 2.0 * half_sin * half_sin, 2.0 * half_sin * half_cos


def split(values):
    high = values.astype(jnp.bfloat16)
    low = (values - high.astype(jnp.float32)).astype(jnp.bfloat16)
    return high, low


def dot(left, right):
    return jnp.dot(left, right, preferred_element_type=jnp.float32)


def dot_rows(left, right):
    return lax.dot_general(
        left, right, (((1,), (1,)), ((), ())), preferred_element_type=jnp.float32
    )


def rows_of(shape):
    return lax.broadcasted_iota(jnp.int32, shape, 0)


def lanes_of(shape):
    return lax.broadcasted_iota(jnp.int32, shape, 1)


def whole(values, divisor):
    return jnp.floor((values + 0.5) * (1.0 / divisor))


def fused_kernel(
    sizes,
    start_smem,
    length_smem,
    column_row,
    length_row,
    coef_ref,
    pot_hbm,
    out_ref,
    line_high,
    line_low,
    send_buf,
    recv_buf,
    ret_buf,
    back_buf,
    pot_vmem,
    combined,
    x_cos,
    x_sin,
    y_up,
    y_down,
    values,
    result,
    pot_sem,
    send_sem,
    recv_sem,
    send_back_sem,
    recv_back_sem,
):
    plane_count, band_count, sub_count, owners, depth, grid, slots, dev_slots, coef_slots, block = sizes
    span = -(-depth // 16) * 16
    devices = plane_count * band_count * sub_count
    half_grid = grid // 2
    wide = y_down.shape[0] // 2

    part = lax.axis_index("parts")
    plane_pos = lax.axis_index("plane")
    band_pos = lax.axis_index("band")
    sub_pos = lax.axis_index("sub")
    me = (plane_pos * band_count + band_pos) * sub_count + sub_pos
    my_owner = plane_pos * sub_count + sub_pos

    def place(step):
        other = lax.rem(me + step, devices)
        other_sub = lax.rem(other, sub_count)
        other_band = lax.rem(other // sub_count, band_count)
        other_plane = other // (sub_count * band_count)
        owner = other_plane * sub_count + other_sub
        return other, owner, other_band, (part, other_plane, other_band, other_sub)

    barrier = pltpu.get_barrier_semaphore()
    for step in range(1, devices):
        pl.semaphore_signal(
            barrier, inc=1, device_id=place(step)[3], device_id_type=pl.DeviceIdType.MESH
        )
    pot_copy = pltpu.make_async_copy(pot_hbm, pot_vmem, pot_sem)
    pot_copy.start()

    def line_block(owner, carry):
        first = start_smem[owner]
        count = start_smem[owner + 1] - first
        shape = (span, coef_slots)
        row = rows_of(shape)
        product = (row + first).astype(jnp.float32) * lanes_of(shape).astype(jnp.float32)
        cos, sin = phases(product, float(grid))
        held = row < count
        cos = jnp.where(held, cos, 0.0)
        sin = jnp.where(held, sin, 0.0)
        blank = jnp.zeros((HALF - span, 2 * coef_slots), jnp.float32)
        rows = jnp.concatenate(
            [
                jnp.concatenate([cos, -sin], axis=1),
                blank,
                jnp.concatenate([sin, cos], axis=1),
                blank,
            ],
            axis=0,
        )
        high, low = split(rows)
        at = pl.ds(pl.multiple_of(owner * LANES, LANES), LANES)
        line_high[at, :] = high
        line_low[at, :] = low
        return carry

    lax.fori_loop(0, owners, line_block, 0, unroll=True)

    lane_small = lanes_of((dev_slots, coef_slots))
    row_small = rows_of((dev_slots, coef_slots))
    own_length = jnp.zeros((dev_slots, coef_slots), jnp.int32)
    for slot in range(dev_slots):
        own_length = jnp.where(row_small == slot, length_smem[me * dev_slots + slot], own_length)
    live = lane_small < own_length
    held = jnp.concatenate(
        [
            jnp.concatenate(
                [jnp.where(live, coef_ref[0, b], 0.0), jnp.where(live, coef_ref[1, b], 0.0)], axis=1
            )
            for b in range(band_count)
        ],
        axis=0,
    )
    high, low = split(held)
    both = dot_rows(jnp.concatenate([high, low], axis=0), line_high[...])
    rows = band_count * dev_slots
    sent = both[:rows] + both[rows:] + dot_rows(high, line_low[...])
    for owner in range(owners):
        for b in range(band_count):
            send_buf[owner, b] = sent[
                b * dev_slots : (b + 1) * dev_slots, owner * LANES : (owner + 1) * LANES
            ]

    pl.semaphore_wait(barrier, devices - 1)

    my_rows = pl.ds(pl.multiple_of(me * dev_slots, dev_slots), dev_slots)

    def outward(step):
        other, owner, band, device = place(step)
        return pltpu.make_async_remote_copy(
            src_ref=send_buf.at[owner, band],
            dst_ref=recv_buf.at[my_rows],
            send_sem=send_sem.at[step - 1],
            recv_sem=recv_sem.at[step - 1],
            device_id=device,
            device_id_type=pl.DeviceIdType.MESH,
        )

    def homeward(step):
        other, owner, band, device = place(step)
        return pltpu.make_async_remote_copy(
            src_ref=ret_buf.at[pl.ds(pl.multiple_of(other * dev_slots, dev_slots), dev_slots)],
            dst_ref=back_buf.at[my_owner, band_pos],
            send_sem=send_back_sem.at[step - 1],
            recv_sem=recv_back_sem.at[step - 1],
            device_id=device,
            device_id_type=pl.DeviceIdType.MESH,
        )

    for step in range(1, devices):
        outward(step).start()
    recv_buf[my_rows, :] = send_buf[my_owner, band_pos]

    column = column_row[...].astype(jnp.float32)
    column_x = whole(column, grid)
    column_y = column - grid * column_x
    cos, sin = phases(rows_of((grid, slots)).astype(jnp.float32) * column_x, float(grid))
    x_cos[...] = cos
    x_sin[...] = sin
    cos, sin = phases(rows_of((wide, slots)).astype(jnp.float32) * column_y, float(grid))
    high, low = split(jnp.concatenate([cos, sin], axis=0))
    y_down[:, :slots] = high
    y_down[:, slots:] = low
    high, low = split(jnp.concatenate([cos.T, sin.T], axis=1))
    y_up[:slots] = high
    y_up[slots : 2 * slots] = high
    y_up[2 * slots :] = low
    half_length = whole(length_row[...].astype(jnp.float32), 2)
    my_first = start_smem[my_owner]
    turn_cos, turn_sin = phases(
        (rows_of((span, slots)) + my_first).astype(jnp.float32) * half_length, float(grid)
    )

    row = rows_of((grid, wide))
    lane = lanes_of((grid, wide))
    same = jnp.where((row == lane) & (lane <= half_grid), 1.0, 0.0)
    mirror = jnp.where((row + lane == grid) & (lane < half_grid), 1.0, 0.0)
    inner = jnp.where((row == lane) & (lane < half_grid) & (lane > 0), 1.0, 0.0)
    pairing = jnp.concatenate([same + mirror, inner - mirror], axis=1).astype(jnp.bfloat16)
    pot_copy.wait()

    def combine(step, carry):
        for i in range(block):
            z = step * block + i
            high, low = split(pot_vmem[z])
            combined[z] = dot(high, pairing) + dot(low, pairing)
        return carry

    lax.fori_loop(0, depth // block, combine, 0)
    result[...] = jnp.zeros_like(result)

    for step in range(1, devices):
        outward(step).wait_recv()
    turned = recv_buf[...].T
    got_real = turned[:span]
    got_imag = turned[HALF : HALF + span]
    values[0] = got_real * turn_cos + got_imag * turn_sin
    values[1] = got_imag * turn_cos - got_real * turn_sin

    def planes(step, carry):
        for i in range(block):
            z = step * block + i
            real = values[0, pl.ds(z, 1), :]
            imag = values[1, pl.ds(z, 1), :]
            ax = x_cos[...]
            bx = x_sin[...]
            high, low = split(
                jnp.concatenate([ax * real - bx * imag, ax * imag + bx * real], axis=0)
            )
            psi = dot(jnp.concatenate([high, low, high], axis=1), y_up[...])
            even_real, odd_real = psi[:grid, :wide], psi[:grid, wide:]
            even_imag, odd_imag = psi[grid:, :wide], psi[grid:, wide:]
            even = combined[z, :, :wide]
            odd = combined[z, :, wide:]
            product = jnp.concatenate(
                [
                    jnp.concatenate(
                        [
                            even * even_real - odd * odd_imag,
                            odd * even_imag + even * odd_real,
                        ],
                        axis=1,
                    ),
                    jnp.concatenate(
                        [
                            even * even_imag + odd * odd_real,
                            even * odd_imag - odd * even_real,
                        ],
                        axis=1,
                    ),
                ],
                axis=0,
            )
            high, low = split(product)
            first = dot(high, y_down[...])
            back = first[:, :slots] + first[:, slots:] + dot(low, y_down[:, :slots])
            back_real, back_imag = back[:grid], back[grid:]
            result[pl.ds(z, 1), :] = jnp.sum(ax * back_real + bx * back_imag, axis=0, keepdims=True)
            result[pl.ds(HALF + z, 1), :] = jnp.sum(
                ax * back_imag - bx * back_real, axis=0, keepdims=True
            )
        return carry

    lax.fori_loop(0, depth // block, planes, 0)

    out_real = result[:span]
    out_imag = result[HALF : HALF + span]
    blank = jnp.zeros((HALF - span, slots), jnp.float32)
    ret_buf[...] = jnp.concatenate(
        [
            out_real * turn_cos - out_imag * turn_sin,
            blank,
            out_imag * turn_cos + out_real * turn_sin,
            blank,
        ],
        axis=0,
    ).T
    for step in range(1, devices):
        homeward(step).start()
    back_buf[my_owner, band_pos] = ret_buf[my_rows, :]
    for step in range(1, devices):
        homeward(step).wait_recv()

    lines = jnp.concatenate(
        [
            jnp.concatenate([back_buf[owner, b] for b in range(band_count)], axis=0)
            for owner in range(owners)
        ],
        axis=1,
    )
    high, low = split(lines)
    both = dot(jnp.concatenate([high, low], axis=0), line_high[...])
    applied = both[:rows] + both[rows:] + dot(high, line_low[...])
    applied = applied * (1.0 / float(grid * grid * grid))
    for b in range(band_count):
        for c in range(2):
            piece = applied[
                b * dev_slots : (b + 1) * dev_slots, c * coef_slots : (c + 1) * coef_slots
            ]
            out_ref[c, b] = jnp.where(live, piece, 0.0)

    for step in range(1, devices):
        outward(step).wait_send()
        homeward(step).wait_send()


def on_device_fused(coefficients, potential, stick_column, stick_length, plane_start):
    plane_count = lax.axis_size("plane")
    band_count = lax.axis_size("band")
    sub_count = lax.axis_size("sub")
    owners = plane_count * sub_count
    depth, grid = potential.shape[0], potential.shape[1]
    dev_slots, coef_slots = coefficients.shape[2], coefficients.shape[3]
    slots = stick_column.shape[0]
    devices = plane_count * band_count * sub_count
    wide = -(-(grid // 2 + 1) // LANES) * LANES
    span = -(-depth // 16) * 16
    block = max(k for k in range(1, 6) if depth % k == 0)
    sizes = (
        plane_count, band_count, sub_count, owners, depth, grid, slots, dev_slots, coef_slots, block
    )
    f32, bf16 = jnp.float32, jnp.bfloat16
    vmem = pl.BlockSpec(memory_space=pltpu.VMEM)
    smem = pl.BlockSpec(memory_space=pltpu.SMEM)
    return pl.pallas_call(
        functools.partial(fused_kernel, sizes),
        out_shape=jax.ShapeDtypeStruct(coefficients.shape, f32),
        in_specs=[smem, smem, vmem, vmem, vmem, pl.BlockSpec(memory_space=pl.ANY)],
        out_specs=vmem,
        scratch_shapes=[
            pltpu.VMEM((owners * LANES, 2 * coef_slots), bf16),
            pltpu.VMEM((owners * LANES, 2 * coef_slots), bf16),
            pltpu.VMEM((owners, band_count, dev_slots, LANES), f32),
            pltpu.VMEM((slots, LANES), f32),
            pltpu.VMEM((slots, LANES), f32),
            pltpu.VMEM((owners, band_count, dev_slots, LANES), f32),
            pltpu.VMEM(potential.shape, f32),
            pltpu.VMEM((depth, grid, 2 * wide), f32),
            pltpu.VMEM((grid, slots), f32),
            pltpu.VMEM((grid, slots), f32),
            pltpu.VMEM((3 * slots, 2 * wide), bf16),
            pltpu.VMEM((2 * wide, 2 * slots), bf16),
            pltpu.VMEM((2, span, slots), f32),
            pltpu.VMEM((LANES, slots), f32),
            pltpu.SemaphoreType.DMA,
            pltpu.SemaphoreType.DMA((devices - 1,)),
            pltpu.SemaphoreType.DMA((devices - 1,)),
            pltpu.SemaphoreType.DMA((devices - 1,)),
            pltpu.SemaphoreType.DMA((devices - 1,)),
        ],
        compiler_params=pltpu.CompilerParams(
            collective_id=0, has_side_effects=True, vmem_limit_bytes=48 * 1024 * 1024
        ),
        cost_estimate=pl.CostEstimate(
            flops=4 * depth * 2 * grid * slots * 2 * wide,
            bytes_accessed=potential.size * 4,
            transcendentals=0,
        ),
    )(
        plane_start,
        stick_length,
        stick_column.reshape(1, slots),
        stick_length.reshape(1, slots),
        coefficients,
        potential,
    )


two_pi = 2.0 * math.pi
precise = lax.Precision.HIGHEST


def phase_table(product, grid_size):
    angle = (product % grid_size).astype(jnp.float32) * (two_pi / grid_size)
    return (jnp.cos(angle), jnp.sin(angle))


def global_slot(owner_src, band_src, within, band_count, sub_count, dev_slots):
    return (
        (owner_src // sub_count * band_count + band_src) * sub_count + owner_src % sub_count
    ) * dev_slots + within


def inverse_columns(parts, lengths, line_cos, line_sin, plane_z, grid_size):
    live_mask = jnp.arange(parts.shape[3], dtype=jnp.int32)[None, :] < lengths[:, None]
    real_part = jnp.where(live_mask, parts[0], 0.0)
    imag_part = jnp.where(live_mask, parts[1], 0.0)
    first_real = jnp.einsum("bsl,lq->bqs", real_part, line_cos, precision=precise) - jnp.einsum(
        "bsl,lq->bqs", imag_part, line_sin, precision=precise
    )
    first_imag = jnp.einsum("bsl,lq->bqs", real_part, line_sin, precision=precise) + jnp.einsum(
        "bsl,lq->bqs", imag_part, line_cos, precision=precise
    )
    shift_cos, shift_sin = phase_table(plane_z[:, None] * (lengths // 2)[None, :], grid_size)
    out_real = first_real * shift_cos + first_imag * shift_sin
    out_imag = first_imag * shift_cos - first_real * shift_sin
    return jnp.stack([out_real, out_imag])


def forward_columns(data, lengths, line_cos, line_sin, plane_z, grid_size):
    shift_cos, shift_sin = phase_table(plane_z[:, None] * (lengths // 2)[None, :], grid_size)
    turn_real = data[0] * shift_cos - data[1] * shift_sin
    turn_imag = data[1] * shift_cos + data[0] * shift_sin
    out_real = jnp.einsum("bqs,lq->bsl", turn_real, line_cos, precision=precise) + jnp.einsum(
        "bqs,lq->bsl", turn_imag, line_sin, precision=precise
    )
    out_imag = jnp.einsum("bqs,lq->bsl", turn_imag, line_cos, precision=precise) - jnp.einsum(
        "bqs,lq->bsl", turn_real, line_sin, precision=precise
    )
    scale = 1.0 / float(grid_size * grid_size * grid_size)
    live_mask = jnp.arange(line_cos.shape[0], dtype=jnp.int32)[None, :] < lengths[:, None]
    return jnp.stack(
        [jnp.where(live_mask, out_real * scale, 0.0), jnp.where(live_mask, out_imag * scale, 0.0)]
    )


def complex_table(dft_cos, dft_sin, sign):
    from_real = jnp.stack([dft_cos, sign * dft_sin], axis=1)
    from_imag = jnp.stack([-sign * dft_sin, dft_cos], axis=1)
    return jnp.stack([from_real, from_imag])


def apply_planes(received, columns, potential, grid_size):
    depth_count = received.shape[1]
    radius = grid_size // 4
    compact = 2 * radius + 1
    col_x = columns // grid_size
    col_y = columns % grid_size
    small_x = jnp.where(col_x <= radius, col_x, col_x - grid_size + compact)
    small_y = jnp.where(col_y <= radius, col_y, col_y - grid_size + compact)
    small_index = small_x * compact + small_y
    spread = (
        jnp.zeros((2, depth_count, compact * compact), jnp.float32)
        .at[:, :, small_index]
        .add(received)
    )
    spread = jnp.transpose(spread.reshape(2, depth_count, compact, compact), (1, 2, 0, 3))
    small_axis = jnp.arange(compact, dtype=jnp.int32)
    wave_freq = jnp.where(small_axis <= radius, small_axis, small_axis - compact + grid_size)
    wave_index = jnp.arange(grid_size, dtype=jnp.int32)
    up_cos, up_sin = phase_table(wave_freq[:, None] * wave_index[None, :], grid_size)
    down_cos, down_sin = phase_table(wave_index[:, None] * wave_freq[None, :], grid_size)
    table_plus = complex_table(up_cos, up_sin, 1.0)
    table_minus = complex_table(down_cos, down_sin, -1.0)
    spread = jnp.einsum("zacb,cadx->zxdb", spread, table_plus, precision=precise)
    spread = jnp.einsum("zxcb,cbdk->zxdk", spread, table_plus, precision=precise)
    spread = spread * potential[:, :, None, :]
    spread = jnp.einsum("zxcy,cydk->zxdk", spread, table_minus, precision=precise)
    spread = jnp.einsum("zxcb,cxda->zadb", spread, table_minus, precision=precise)
    planes_flat = jnp.transpose(spread, (2, 0, 1, 3)).reshape(2, depth_count, compact * compact)
    return planes_flat[:, :, small_index]


def on_device(coefficients, potential, stick_column, stick_length, plane_start):
    plane_count = lax.axis_size("plane")
    band_count = lax.axis_size("band")
    sub_count = lax.axis_size("sub")
    owners_count = plane_count * sub_count
    plane_depth = potential.shape[0]
    grid_size = potential.shape[1]
    coef_slots = coefficients.shape[3]
    dev_slots = coefficients.shape[2]
    group_slots = band_count * dev_slots
    plane_pos = lax.axis_index("plane")
    sub_pos = lax.axis_index("sub")
    my_owner = plane_pos * sub_count + sub_pos
    plane_counts = plane_start[1:] - plane_start[:-1]
    depth_index = jnp.arange(plane_depth, dtype=jnp.int32)
    valid_plane = (depth_index[None, :] < plane_counts[:, None]).reshape(-1)
    plane_z = jnp.where(
        valid_plane, (plane_start[:-1][:, None] + depth_index[None, :]).reshape(-1), 0
    )
    line_index = jnp.arange(coef_slots, dtype=jnp.int32)
    line_cos, line_sin = phase_table(line_index[:, None] * plane_z[None, :], grid_size)
    valid_float = valid_plane.astype(jnp.float32)[None, :]
    line_cos = line_cos * valid_float
    line_sin = line_sin * valid_float
    owner_axis = jnp.arange(owners_count, dtype=jnp.int32)
    band_axis = jnp.arange(band_count, dtype=jnp.int32)
    within_axis = jnp.arange(dev_slots, dtype=jnp.int32)
    owner_major = global_slot(
        owner_axis[:, None, None],
        band_axis[None, :, None],
        within_axis[None, None, :],
        band_count,
        sub_count,
        dev_slots,
    ).reshape(-1)
    total_slots = owner_major.shape[0]
    question = plane_depth * owners_count
    group_ids = global_slot(
        my_owner, band_axis[:, None], within_axis[None, :], band_count, sub_count, dev_slots
    ).reshape(-1)
    group_len = stick_length[group_ids]
    regrouped = lax.all_to_all(coefficients, "band", split_axis=1, concat_axis=2, tiled=True)
    columns_z = inverse_columns(regrouped, group_len, line_cos, line_sin, plane_z, grid_size)
    columns_z = columns_z.reshape(2, 1, owners_count, plane_depth, group_slots)
    arrived = lax.all_to_all(columns_z, ("plane", "sub"), split_axis=2, concat_axis=4, tiled=True)
    planes_out = apply_planes(
        arrived.reshape(2, plane_depth, total_slots),
        stick_column[owner_major],
        potential,
        grid_size,
    )
    returned = lax.all_to_all(
        planes_out.reshape(2, 1, 1, plane_depth, total_slots),
        ("plane", "sub"),
        split_axis=4,
        concat_axis=2,
        tiled=True,
    )
    coef_back = forward_columns(
        returned.reshape(2, 1, question, group_slots),
        group_len,
        line_cos,
        line_sin,
        plane_z,
        grid_size,
    )
    applied = lax.all_to_all(coef_back, "band", split_axis=2, concat_axis=1, tiled=True)
    return applied


def on_device_any(coefficients, potential, stick_column, stick_length, plane_start):
    small = (
        stick_column.shape[0] <= 512 and potential.shape[0] <= HALF and coefficients.shape[2] == 8
    )
    chosen = on_device_fused if small else on_device
    return chosen(coefficients, potential, stick_column, stick_length, plane_start)


def solution(mesh):
    placed = (
        P(None, None, ("parts", "plane", "band", "sub"), None),
        P(("parts", "plane", "sub"), None, None),
        P(),
        P(),
        P(),
    )
    return jax.shard_map(
        on_device_any,
        mesh=mesh,
        in_specs=placed,
        out_specs=P(None, None, ("parts", "plane", "band", "sub"), None),
        check_vma=False,
    )
```

profile of v0, /device:TPU:0, one launch (start us, length us, event | category | flops | bytes accessed | tf_op | source)
XLA Modules:
  0.0 29.3 jit_solution(11656845223585090299)
XLA Ops:
  0.0 0.0 copy-start
  0.0 2.4 %copy-done = f32[25,192,192]{2,1,0:T(8,128)S(1)} copy-done((f32[25,192,192]{2,1,0:T(8,128)S(1)}, f32[25,192,192]{2,1,0:T(8,128)}, u32[]{:S(2)}) %copy-start) | copy-done | bytes 3686424
  2.4 0.0 copy-start.1
  2.4 0.7 %copy-done.1 = f32[2,2,8,128]{3,2,1,0:T(8,128)S(1)} copy-done((f32[2,2,8,128]{3,2,1,0:T(8,128)S(1)}, f32[2,2,8,128]{3,2,1,0:T(8,128)}, u32[]{:S(2)}) %copy-start.1) | copy-done | bytes 16408
  3.1 0.0 copy-start.2
  3.1 0.7 %copy-done.2 = s32[128]{0:T(128)S(1)} copy-done((s32[128]{0:T(128)S(1)}, s32[128]{0:T(128)}, u32[]{:S(2)}) %copy-start.2) | copy-done | bytes 536
  3.8 0.0 copy-start.3
  3.8 0.7 %copy-done.3 = s32[9]{0:T(128)S(1)} copy-done((s32[9]{0:T(128)S(1)}, s32[9]{0:T(128)}, u32[]{:S(2)}) %copy-start.3) | copy-done | bytes 60
  4.4 0.0 copy-start.4
  4.4 0.7 %copy-done.4 = s32[128]{0:T(128)S(1)} copy-done((s32[128]{0:T(128)S(1)}, s32[128]{0:T(128)}, u32[]{:S(2)}) %copy-start.4) | copy-done | bytes 536
  5.1 23.7 %shard_map.55 = f32[2,2,8,128]{3,2,1,0:T(8,128)S(1)} custom-call(s32[9]{0:T(128)S(1)} %copy-done.3, s32[128]{0:T(128)S(1)} %copy-done.2, s32[1,128]{1,0:T(1,128)S(1)} %bitcast.3, s32[1,128]{1,0:T(1,128)S(1)} %bitcast.2, f32[2,2,8,128]{3,2,1,0:T(8,128)S(1)} %copy-done.1, f32[25,192,192]{2,1,0:T(8,128)S(1)} %copy-done), custom_call_target="tpu_custom_call" | custom-call | flops 1258291200 | bytes 3686400 | tf_op jit(solution)/shard_map/pallas_call | solution.py:354
  28.7 0.6 %copy.7 = f32[2,2,8,128]{3,2,1,0:T(8,128)} copy(f32[2,2,8,128]{3,2,1,0:T(8,128)S(1)} %shard_map.55) | data formatting | bytes 32768
Async XLA Ops:
  0.0 2.4 %copy-start = (f32[25,192,192]{2,1,0:T(8,128)S(1)}, f32[25,192,192]{2,1,0:T(8,128)}, u32[]{:S(2)}) copy-start(f32[25,192,192]{2,1,0:T(8,128)} %pot_hbm.1) | copy-start | bytes 11059204
  2.4 0.7 %copy-start.1 = (f32[2,2,8,128]{3,2,1,0:T(8,128)S(1)}, f32[2,2,8,128]{3,2,1,0:T(8,128)}, u32[]{:S(2)}) copy-start(f32[2,2,8,128]{3,2,1,0:T(8,128)} %coef_ref.1) | copy-start | bytes 49156
  3.1 0.7 %copy-start.2 = (s32[128]{0:T(128)S(1)}, s32[128]{0:T(128)}, u32[]{:S(2)}) copy-start(s32[128]{0:T(128)} %length_smem.1) | copy-start | bytes 1540
  3.8 0.7 %copy-start.3 = (s32[9]{0:T(128)S(1)}, s32[9]{0:T(128)}, u32[]{:S(2)}) copy-start(s32[9]{0:T(128)} %start_smem.1) | copy-start | bytes 112
  4.4 0.7 %copy-start.4 = (s32[128]{0:T(128)S(1)}, s32[128]{0:T(128)}, u32[]{:S(2)}) copy-start(s32[128]{0:T(128)} %param.7) | copy-start | bytes 1540
where the time goes:
time: 29.6 us; the launch traced here: 29.3 us
  Pallas kernels  23.7 us (80%)
  local copies, waits for them, and re-layouts  5.68 us (19%)
    pallas_call x1, Pallas kernels, on_device_fused(): pl.pallas_call(functools.partial(fused_kernel, sizes), out_shape=jax.Shap...  23.7 us
    unnamed x11, local copies, waits for them, and re-layouts  5.68 us

commit v1 on v0

--- a/solution.py
+++ b/solution.py
@@ -61,13 +61,18 @@
 
 def fused_kernel(
     sizes,
+    start_hbm,
+    length_hbm,
+    column_row_hbm,
+    length_row_hbm,
+    coef_hbm,
+    pot_hbm,
+    out_ref,
     start_smem,
     length_smem,
     column_row,
     length_row,
     coef_ref,
-    pot_hbm,
-    out_ref,
     line_high,
     line_low,
     send_buf,
@@ -83,10 +88,9 @@
     values,
     result,
     pot_sem,
-    send_sem,
-    recv_sem,
-    send_back_sem,
-    recv_back_sem,
+    small_sem,
+    out_sems,
+    home_sems,
 ):
     plane_count, band_count, sub_count, owners, depth, grid, slots, dev_slots, coef_slots, block = sizes
     span = -(-depth // 16) * 16
@@ -101,21 +105,53 @@
     me = (plane_pos * band_count + band_pos) * sub_count + sub_pos
     my_owner = plane_pos * sub_count + sub_pos
 
+    def wrap(position, offset, count):
+        moved = position + offset
+        return jnp.where(moved >= count, moved - count, moved)
+
     def place(step):
-        other = lax.rem(me + step, devices)
-        other_sub = lax.rem(other, sub_count)
-        other_band = lax.rem(other // sub_count, band_count)
-        other_plane = other // (sub_count * band_count)
+        other_plane = wrap(plane_pos, step[0], plane_count)
+        other_band = wrap(band_pos, step[1], band_count)
+        other_sub = wrap(sub_pos, step[2], sub_count)
         owner = other_plane * sub_count + other_sub
-        return other, owner, other_band, (part, other_plane, other_band, other_sub)
-
+        other = (other_plane * band_count + other_band) * sub_count + other_sub
+        tile = owner * band_count + other_band
+        return other, tile, (part, other_plane, other_band, other_sub)
+
+    steps = [
+        (p, b, s)
+        for p in sorted(range(plane_count), key=lambda p: -min(p, plane_count - p))
+        for b in reversed(range(band_count))
+        for s in reversed(range(sub_count))
+        if p + b + s > 0
+    ]
+    places = [place(step) for step in steps]
+    my_tile = my_owner * band_count + band_pos
+
+    small_copies = [
+        pltpu.make_async_copy(source, target, small_sem.at[i])
+        for i, (source, target) in enumerate(
+            [
+                (start_hbm, start_smem),
+                (length_hbm, length_smem),
+                (coef_hbm, coef_ref),
+                (column_row_hbm, column_row),
+                (length_row_hbm, length_row),
+            ]
+        )
+    ]
+    for copy in small_copies:
+        copy.start()
     barrier = pltpu.get_barrier_semaphore()
-    for step in range(1, devices):
+    for _, _, device in places:
         pl.semaphore_signal(
-            barrier, inc=1, device_id=place(step)[3], device_id_type=pl.DeviceIdType.MESH
+            barrier, inc=1, device_id=device, device_id_type=pl.DeviceIdType.MESH
         )
     pot_copy = pltpu.make_async_copy(pot_hbm, pot_vmem, pot_sem)
     pot_copy.start()
+
+    for copy in small_copies:
+        copy.wait()
 
     def line_block(owner, carry):
         first = start_smem[owner]
@@ -166,39 +202,29 @@
     sent = both[:rows] + both[rows:] + dot_rows(high, line_low[...])
     for owner in range(owners):
         for b in range(band_count):
-            send_buf[owner, b] = sent[
+            send_buf[owner * band_count + b] = sent[
                 b * dev_slots : (b + 1) * dev_slots, owner * LANES : (owner + 1) * LANES
             ]
 
     pl.semaphore_wait(barrier, devices - 1)
 
-    my_rows = pl.ds(pl.multiple_of(me * dev_slots, dev_slots), dev_slots)
-
-    def outward(step):
-        other, owner, band, device = place(step)
+    def send(source, target, sems, device):
         return pltpu.make_async_remote_copy(
-            src_ref=send_buf.at[owner, band],
-            dst_ref=recv_buf.at[my_rows],
-            send_sem=send_sem.at[step - 1],
-            recv_sem=recv_sem.at[step - 1],
+            src_ref=source,
+            dst_ref=target,
+            send_sem=sems.at[0],
+            recv_sem=sems.at[1],
             device_id=device,
             device_id_type=pl.DeviceIdType.MESH,
         )
 
-    def homeward(step):
-        other, owner, band, device = place(step)
-        return pltpu.make_async_remote_copy(
-            src_ref=ret_buf.at[pl.ds(pl.multiple_of(other * dev_slots, dev_slots), dev_slots)],
-            dst_ref=back_buf.at[my_owner, band_pos],
-            send_sem=send_back_sem.at[step - 1],
-            recv_sem=recv_back_sem.at[step - 1],
-            device_id=device,
-            device_id_type=pl.DeviceIdType.MESH,
-        )
-
-    for step in range(1, devices):
-        outward(step).start()
-    recv_buf[my_rows, :] = send_buf[my_owner, band_pos]
+    def all_of(buffer, sems):
+        others = buffer.at[pl.ds(0, devices - 1)]
+        return send(others, others, sems, places[0][2])
+
+    for _, tile, device in places:
+        send(send_buf.at[tile], recv_buf.at[me], out_sems, device).start()
+    recv_buf[me] = send_buf[my_tile]
 
     column = column_row[...].astype(jnp.float32)
     column_x = whole(column, grid)
@@ -238,9 +264,8 @@
     lax.fori_loop(0, depth // block, combine, 0)
     result[...] = jnp.zeros_like(result)
 
-    for step in range(1, devices):
-        outward(step).wait_recv()
-    turned = recv_buf[...].T
+    all_of(recv_buf, out_sems).wait_recv()
+    turned = recv_buf[...].reshape(slots, LANES).T
     got_real = turned[:span]
     got_imag = turned[HALF : HALF + span]
     values[0] = got_real * turn_cos + got_imag * turn_sin
@@ -303,16 +328,15 @@
             blank,
         ],
         axis=0,
-    ).T
-    for step in range(1, devices):
-        homeward(step).start()
-    back_buf[my_owner, band_pos] = ret_buf[my_rows, :]
-    for step in range(1, devices):
-        homeward(step).wait_recv()
+    ).T.reshape(devices, dev_slots, LANES)
+    for other, _, device in places:
+        send(ret_buf.at[other], back_buf.at[my_tile], home_sems, device).start()
+    back_buf[my_tile] = ret_buf[me]
+    all_of(back_buf, home_sems).wait_recv()
 
     lines = jnp.concatenate(
         [
-            jnp.concatenate([back_buf[owner, b] for b in range(band_count)], axis=0)
+            jnp.concatenate([back_buf[owner * band_count + b] for b in range(band_count)], axis=0)
             for owner in range(owners)
         ],
         axis=1,
@@ -328,9 +352,8 @@
             ]
             out_ref[c, b] = jnp.where(live, piece, 0.0)
 
-    for step in range(1, devices):
-        outward(step).wait_send()
-        homeward(step).wait_send()
+    all_of(send_buf, out_sems).wait_send()
+    all_of(ret_buf, home_sems).wait_send()
 
 
 def on_device_fused(coefficients, potential, stick_column, stick_length, plane_start):
@@ -350,19 +373,23 @@
     )
     f32, bf16 = jnp.float32, jnp.bfloat16
     vmem = pl.BlockSpec(memory_space=pltpu.VMEM)
-    smem = pl.BlockSpec(memory_space=pltpu.SMEM)
     return pl.pallas_call(
         functools.partial(fused_kernel, sizes),
         out_shape=jax.ShapeDtypeStruct(coefficients.shape, f32),
-        in_specs=[smem, smem, vmem, vmem, vmem, pl.BlockSpec(memory_space=pl.ANY)],
+        in_specs=[pl.BlockSpec(memory_space=pltpu.HBM)] * 6,
         out_specs=vmem,
         scratch_shapes=[
+            pltpu.SMEM(plane_start.shape, jnp.int32),
+            pltpu.SMEM(stick_length.shape, jnp.int32),
+            pltpu.VMEM((1, slots), jnp.int32),
+            pltpu.VMEM((1, slots), jnp.int32),
+            pltpu.VMEM(coefficients.shape, f32),
             pltpu.VMEM((owners * LANES, 2 * coef_slots), bf16),
             pltpu.VMEM((owners * LANES, 2 * coef_slots), bf16),
-            pltpu.VMEM((owners, band_count, dev_slots, LANES), f32),
-            pltpu.VMEM((slots, LANES), f32),
-            pltpu.VMEM((slots, LANES), f32),
-            pltpu.VMEM((owners, band_count, dev_slots, LANES), f32),
+            pltpu.VMEM((devices, dev_slots, LANES), f32),
+            pltpu.VMEM((devices, dev_slots, LANES), f32),
+            pltpu.VMEM((devices, dev_slots, LANES), f32),
+            pltpu.VMEM((devices, dev_slots, LANES), f32),
             pltpu.VMEM(potential.shape, f32),
             pltpu.VMEM((depth, grid, 2 * wide), f32),
             pltpu.VMEM((grid, slots), f32),
@@ -372,13 +399,12 @@
             pltpu.VMEM((2, span, slots), f32),
             pltpu.VMEM((LANES, slots), f32),
             pltpu.SemaphoreType.DMA,
-            pltpu.SemaphoreType.DMA((devices - 1,)),
-            pltpu.SemaphoreType.DMA((devices - 1,)),
-            pltpu.SemaphoreType.DMA((devices - 1,)),
-            pltpu.SemaphoreType.DMA((devices - 1,)),
+            pltpu.SemaphoreType.DMA((5,)),
+            pltpu.SemaphoreType.DMA((2,)),
+            pltpu.SemaphoreType.DMA((2,)),
         ],
         compiler_params=pltpu.CompilerParams(
-            collective_id=0, has_side_effects=True, vmem_limit_bytes=48 * 1024 * 1024
+            collective_id=0, has_side_effects=True, vmem_limit_bytes=64 * 1024 * 1024
         ),
         cost_estimate=pl.CostEstimate(
             flops=4 * depth * 2 * grid * slots * 2 * wide,

time: 29.6 us -> 24.9 us (0.84)
  local copies, waits for them, and re-layouts: 5.68 us -> 1.32 us
  Pallas kernels: 23.7 us -> 23.3 us
    unnamed x11 -> x1, local copies, waits for them, and re-layouts: 5.68 us -> 1.32 us
    pallas_call x1, Pallas kernels: 23.7 us -> 23.3 us  [on_device_fused(): pl.pallas_call(functools.partial(fused_kernel, sizes), out_shape=jax.Shap...]
where the time goes in v1:
time: 24.9 us; the launch traced here: 24.7 us
  Pallas kernels  23.3 us (94%)
  local copies, waits for them, and re-layouts  1.32 us (5%)
    pallas_call x1, Pallas kernels, on_device_fused(): pl.pallas_call(functools.partial(fused_kernel, sizes), out_shape=jax.Shap...  23.3 us
    unnamed x1, local copies, waits for them, and re-layouts  1.32 us

profile of v1, /device:TPU:0, one launch (start us, length us, event | category | flops | bytes accessed | tf_op | source)
XLA Modules:
  0.0 24.7 jit_solution(8736540259794733138)
XLA Ops:
  0.0 23.3 %shard_map.55 = f32[2,2,8,128]{3,2,1,0:T(8,128)} custom-call(s32[9]{0:T(128)} %start_hbm.1, s32[128]{0:T(128)} %length_hbm.1, s32[1,128]{1,0:T(1,128)} %bitcast.3, s32[1,128]{1,0:T(1,128)} %bitcast.2, f32[2,2,8,128]{3,2,1,0:T(8,128)} %coef_hbm.1, f32[25,192,192]{2,1,0:T(8,128)} %pot_hbm.1), custom_call_target="tpu_custom_call" | custom-call | flops 1258291200 | bytes 3686400 | tf_op jit(solution)/shard_map/pallas_call | solution.py:376
  23.3 1.3 %copy.7 = f32[2,2,8,128]{3,2,1,0:T(8,128)} copy(f32[2,2,8,128]{3,2,1,0:T(8,128)} %shard_map.55) | data formatting | bytes 32768

commit v2 on v1

--- a/solution.py
+++ b/solution.py
@@ -272,8 +272,8 @@
     values[1] = got_imag * turn_cos - got_real * turn_sin
 
     def planes(step, carry):
-        for i in range(block):
-            z = step * block + i
+        for i in range(depth):
+            z = i
             real = values[0, pl.ds(z, 1), :]
             imag = values[1, pl.ds(z, 1), :]
             ax = x_cos[...]
@@ -315,7 +315,7 @@
             )
         return carry
 
-    lax.fori_loop(0, depth // block, planes, 0)
+    planes(0, 0)
 
     out_real = result[:span]
     out_imag = result[HALF : HALF + span]

time: 24.9 us -> 23.1 us (0.928)
  Pallas kernels: 23.3 us -> 21.5 us
    pallas_call x1, Pallas kernels: 23.3 us -> 21.5 us  [on_device_fused(): pl.pallas_call(functools.partial(fused_kernel, sizes), out_shape=jax.Shap...]
where the time goes in v2:
time: 23.1 us; the launch traced here: 22.9 us
  Pallas kernels  21.5 us (93%)
  local copies, waits for them, and re-layouts  1.32 us (6%)
    pallas_call x1, Pallas kernels, on_device_fused(): pl.pallas_call(functools.partial(fused_kernel, sizes), out_shape=jax.Shap...  21.5 us
    unnamed x1, local copies, waits for them, and re-layouts  1.32 us

profile of v2, /device:TPU:0, one launch (start us, length us, event | category | flops | bytes accessed | tf_op | source)
XLA Modules:
  0.0 22.9 jit_solution(12029114121173865922)
XLA Ops:
  0.0 21.5 %shard_map.55 = f32[2,2,8,128]{3,2,1,0:T(8,128)} custom-call(s32[9]{0:T(128)} %start_hbm.1, s32[128]{0:T(128)} %length_hbm.1, s32[1,128]{1,0:T(1,128)} %bitcast.3, s32[1,128]{1,0:T(1,128)} %bitcast.2, f32[2,2,8,128]{3,2,1,0:T(8,128)} %coef_hbm.1, f32[25,192,192]{2,1,0:T(8,128)} %pot_hbm.1), custom_call_target="tpu_custom_call" | custom-call | flops 1258291200 | bytes 3686400 | tf_op jit(solution)/shard_map/pallas_call | solution.py:376
  21.6 1.3 %copy.7 = f32[2,2,8,128]{3,2,1,0:T(8,128)} copy(f32[2,2,8,128]{3,2,1,0:T(8,128)} %shard_map.55) | data formatting | bytes 32768

commit v3 on v2

--- a/solution.py
+++ b/solution.py
@@ -271,51 +271,49 @@
     values[0] = got_real * turn_cos + got_imag * turn_sin
     values[1] = got_imag * turn_cos - got_real * turn_sin
 
-    def planes(step, carry):
-        for i in range(depth):
-            z = i
+    def planes(first):
+        ax = x_cos[...]
+        bx = x_sin[...]
+        group = range(first, first + block)
+        parts = []
+        for z in group:
             real = values[0, pl.ds(z, 1), :]
             imag = values[1, pl.ds(z, 1), :]
-            ax = x_cos[...]
-            bx = x_sin[...]
-            high, low = split(
-                jnp.concatenate([ax * real - bx * imag, ax * imag + bx * real], axis=0)
-            )
-            psi = dot(jnp.concatenate([high, low, high], axis=1), y_up[...])
+            parts += [ax * real - bx * imag, ax * imag + bx * real]
+        high, low = split(jnp.concatenate(parts, axis=0))
+        both_psi = dot(jnp.concatenate([high, low, high], axis=1), y_up[...])
+        parts = []
+        for i, z in enumerate(group):
+            psi = both_psi[2 * i * grid : 2 * (i + 1) * grid]
             even_real, odd_real = psi[:grid, :wide], psi[:grid, wide:]
             even_imag, odd_imag = psi[grid:, :wide], psi[grid:, wide:]
             even = combined[z, :, :wide]
             odd = combined[z, :, wide:]
-            product = jnp.concatenate(
-                [
-                    jnp.concatenate(
-                        [
-                            even * even_real - odd * odd_imag,
-                            odd * even_imag + even * odd_real,
-                        ],
-                        axis=1,
-                    ),
-                    jnp.concatenate(
-                        [
-                            even * even_imag + odd * odd_real,
-                            even * odd_imag - odd * even_real,
-                        ],
-                        axis=1,
-                    ),
-                ],
-                axis=0,
-            )
-            high, low = split(product)
-            first = dot(high, y_down[...])
-            back = first[:, :slots] + first[:, slots:] + dot(low, y_down[:, :slots])
-            back_real, back_imag = back[:grid], back[grid:]
+            product_real = [
+                even * even_real - odd * odd_imag,
+                odd * even_imag + even * odd_real,
+            ]
+            product_imag = [
+                even * even_imag + odd * odd_real,
+                even * odd_imag - odd * even_real,
+            ]
+            parts += [
+                jnp.concatenate(product_real, axis=1),
+                jnp.concatenate(product_imag, axis=1),
+            ]
+        high, low = split(jnp.concatenate(parts, axis=0))
+        once = dot(high, y_down[...])
+        back = once[:, :slots] + once[:, slots:] + dot(low, y_down[:, :slots])
+        for i, z in enumerate(group):
+            back_real = back[2 * i * grid : (2 * i + 1) * grid]
+            back_imag = back[(2 * i + 1) * grid : 2 * (i + 1) * grid]
             result[pl.ds(z, 1), :] = jnp.sum(ax * back_real + bx * back_imag, axis=0, keepdims=True)
             result[pl.ds(HALF + z, 1), :] = jnp.sum(
                 ax * back_imag - bx * back_real, axis=0, keepdims=True
             )
-        return carry
-
-    planes(0, 0)
+
+    for first in range(0, depth, block):
+        planes(first)
 
     out_real = result[:span]
     out_imag = result[HALF : HALF + span]

time: 23.1 us -> 24.1 us (1.043)
  Pallas kernels: 21.5 us -> 22.5 us
    pallas_call x1, Pallas kernels: 21.5 us -> 22.5 us  [on_device_fused(): pl.pallas_call(functools.partial(fused_kernel, sizes), out_shape=jax.Shap...]
where the time goes in v3:
time: 24.1 us; the launch traced here: 23.9 us
  Pallas kernels  22.5 us (93%)
  local copies, waits for them, and re-layouts  1.32 us (5%)
    pallas_call x1, Pallas kernels, on_device_fused(): pl.pallas_call(functools.partial(fused_kernel, sizes), out_shape=jax.Shap...  22.5 us
    unnamed x1, local copies, waits for them, and re-layouts  1.32 us

profile of v3, /device:TPU:0, one launch (start us, length us, event | category | flops | bytes accessed | tf_op | source)
XLA Modules:
  0.0 23.9 jit_solution(11360424358730562827)
XLA Ops:
  0.0 22.5 %shard_map.55 = f32[2,2,8,128]{3,2,1,0:T(8,128)} custom-call(s32[9]{0:T(128)} %start_hbm.1, s32[128]{0:T(128)} %length_hbm.1, s32[1,128]{1,0:T(1,128)} %bitcast.3, s32[1,128]{1,0:T(1,128)} %bitcast.2, f32[2,2,8,128]{3,2,1,0:T(8,128)} %coef_hbm.1, f32[25,192,192]{2,1,0:T(8,128)} %pot_hbm.1), custom_call_target="tpu_custom_call" | custom-call | flops 1258291200 | bytes 3686400 | tf_op jit(solution)/shard_map/pallas_call | solution.py:374
  22.6 1.3 %copy.7 = f32[2,2,8,128]{3,2,1,0:T(8,128)} copy(f32[2,2,8,128]{3,2,1,0:T(8,128)} %shard_map.55) | data formatting | bytes 32768

commit v4 on v2

--- a/solution.py
+++ b/solution.py
@@ -206,26 +206,6 @@
                 b * dev_slots : (b + 1) * dev_slots, owner * LANES : (owner + 1) * LANES
             ]
 
-    pl.semaphore_wait(barrier, devices - 1)
-
-    def send(source, target, sems, device):
-        return pltpu.make_async_remote_copy(
-            src_ref=source,
-            dst_ref=target,
-            send_sem=sems.at[0],
-            recv_sem=sems.at[1],
-            device_id=device,
-            device_id_type=pl.DeviceIdType.MESH,
-        )
-
-    def all_of(buffer, sems):
-        others = buffer.at[pl.ds(0, devices - 1)]
-        return send(others, others, sems, places[0][2])
-
-    for _, tile, device in places:
-        send(send_buf.at[tile], recv_buf.at[me], out_sems, device).start()
-    recv_buf[me] = send_buf[my_tile]
-
     column = column_row[...].astype(jnp.float32)
     column_x = whole(column, grid)
     column_y = column - grid * column_x
@@ -245,6 +225,26 @@
     turn_cos, turn_sin = phases(
         (rows_of((span, slots)) + my_first).astype(jnp.float32) * half_length, float(grid)
     )
+
+    pl.semaphore_wait(barrier, devices - 1)
+
+    def send(source, target, sems, device):
+        return pltpu.make_async_remote_copy(
+            src_ref=source,
+            dst_ref=target,
+            send_sem=sems.at[0],
+            recv_sem=sems.at[1],
+            device_id=device,
+            device_id_type=pl.DeviceIdType.MESH,
+        )
+
+    def all_of(buffer, sems):
+        others = buffer.at[pl.ds(0, devices - 1)]
+        return send(others, others, sems, places[0][2])
+
+    for _, tile, device in places:
+        send(send_buf.at[tile], recv_buf.at[me], out_sems, device).start()
+    recv_buf[me] = send_buf[my_tile]
 
     row = rows_of((grid, wide))
     lane = lanes_of((grid, wide))

time: 23.1 us -> 23.1 us (level)
  no operation moved by 1% of the time
where the time goes in v4:
time: 23.1 us; the launch traced here: 22.9 us
  Pallas kernels  21.5 us (93%)
  local copies, waits for them, and re-layouts  1.32 us (6%)
    pallas_call x1, Pallas kernels, on_device_fused(): pl.pallas_call(functools.partial(fused_kernel, sizes), out_shape=jax.Shap...  21.5 us
    unnamed x1, local copies, waits for them, and re-layouts  1.32 us

profile of v4, /device:TPU:0, one launch (start us, length us, event | category | flops | bytes accessed | tf_op | source)
XLA Modules:
  0.0 22.9 jit_solution(17389398037464921018)
XLA Ops:
  0.0 21.5 %shard_map.55 = f32[2,2,8,128]{3,2,1,0:T(8,128)} custom-call(s32[9]{0:T(128)} %start_hbm.1, s32[128]{0:T(128)} %length_hbm.1, s32[1,128]{1,0:T(1,128)} %bitcast.3, s32[1,128]{1,0:T(1,128)} %bitcast.2, f32[2,2,8,128]{3,2,1,0:T(8,128)} %coef_hbm.1, f32[25,192,192]{2,1,0:T(8,128)} %pot_hbm.1), custom_call_target="tpu_custom_call" | custom-call | flops 1258291200 | bytes 3686400 | tf_op jit(solution)/shard_map/pallas_call | solution.py:376
  21.6 1.3 %copy.7 = f32[2,2,8,128]{3,2,1,0:T(8,128)} copy(f32[2,2,8,128]{3,2,1,0:T(8,128)} %shard_map.55) | data formatting | bytes 32768
